TPU v7x, 256 devices: a whole 4x4x8 slice. The times are simulated.
256 devices in a mesh: ctx: 32 (over z, x_hi, core), tp: 8 (over x_lo, y).
Axes of the slice: x: 4 (x_hi: 2, x_lo: 2; x = x_hi * 2 + x_lo), y: 4, z: 8, core: 2. Of those that a mesh axis runs over, the one named last changes fastest.
Arguments:
- layer_input_rows: bfloat16 [32768, 4608], P('ctx', 'tp'), may hold values from -6 to 6
- queries: bfloat16 [32768, 2048], P('ctx', 'tp'), may hold values from -6 to 6
- keys: bfloat16 [32768, 1024], P('ctx', 'tp'), may hold values from -6 to 6
- values: bfloat16 [32768, 1024], P('ctx', 'tp'), may hold values from -6 to 6
- output_gradient: bfloat16 [32768, 2048], P('ctx', 'tp'), may hold values from -6 to 6
- outputs: bfloat16 [32768, 2048], P('ctx', 'tp'), may hold values from -6 to 6
- softmax_log_totals: float32 [16, 32768], P('tp', 'ctx'), may hold values from 3 to 5
- token_document_index: int32 [32768], P('ctx'), may hold values from 0 to 3, never falling along the last dimension, each value on 1 to 16384 neighbouring positions
- query_adapter_down_weight: bfloat16 [4608, 128], P('tp'), may hold values from -0.09375 to 0.09375
- query_adapter_up_weight: bfloat16 [128, 2048], P(None, 'tp'), may hold values from -0.125 to 0.125
- value_adapter_down_weight: bfloat16 [4608, 128], P('tp'), may hold values from -0.09375 to 0.09375
- value_adapter_up_weight: bfloat16 [128, 1024], P(None, 'tp'), may hold values from -0.1875 to 0.1875
Outputs:
- key_grad: bfloat16 [32768, 1024], P('ctx', 'tp')
- grad_a_query: float32 [4608, 128], P('tp')
- grad_b_query: float32 [128, 2048], P(None, 'tp')
- grad_a_value: float32 [4608, 128], P('tp')
- grad_b_value: float32 [128, 1024], P(None, 'tp')
Inputs may be any that keep to these rules, and one draw needn't show every extreme that they name: `token_document_index`: ids never fall along the tokens; each document holds 1 to 16384 tokens and one holds exactly 16384.
All inputs are finite; a program needn't handle non-finite values.
Results may differ from a plain program's by a relative error of at most 0.0058.
Values may be sent and summed in bfloat16 or wider, within the bound.
A program may use at most 128 MiB of HBM per device.

v0:
```python
import math

import jax
import jax.numpy as jnp
from jax import lax
from jax.sharding import PartitionSpec as P

QUERY_HEADS = 16
KEY_VALUE_HEADS = 8
HEAD_WIDTH = 128
WINDOW = 4096


SCORE_SCALE = 144.0 ** (-0.5)


def passed_along(value, axis, steps):
    count = lax.axis_size(axis)
    first, last = (max(0, -steps), min(count, count - steps))
    return lax.ppermute(value, axis, [(source, source + steps) for source in range(first, last)])


def per_device(
    layer_input_rows,
    queries,
    keys,
    values,
    output_gradient,
    outputs,
    softmax_log_totals,
    token_document_index,
    query_adapter_down_weight,
    query_adapter_up_weight,
    value_adapter_down_weight,
    value_adapter_up_weight,
):
    tok_rows = queries.shape[0]
    kv_local = keys.shape[1] // HEAD_WIDTH
    q_group = QUERY_HEADS // KEY_VALUE_HEADS
    reach_count = WINDOW // tok_rows
    my_place = lax.axis_index("ctx")
    query_heads = queries.reshape(tok_rows, kv_local, q_group, HEAD_WIDTH)
    grad_heads = output_gradient.reshape(tok_rows, kv_local, q_group, HEAD_WIDTH)
    out_heads = outputs.reshape(tok_rows, kv_local, q_group, HEAD_WIDTH)
    row_delta = jnp.einsum(
        "ikgd,ikgd->kgi", grad_heads, out_heads, preferred_element_type=jnp.float32
    )
    normalizer = softmax_log_totals.reshape(kv_local, q_group, tok_rows)
    offsets = jnp.arange(tok_rows, dtype=jnp.int32)
    query_low_rank_output = jnp.dot(
        layer_input_rows, query_adapter_down_weight, preferred_element_type=jnp.float32
    )
    value_low_rank_output = jnp.dot(
        layer_input_rows, value_adapter_down_weight, preferred_element_type=jnp.float32
    )
    adapter_input_list = lax.psum((query_low_rank_output, value_low_rank_output), "tp")
    own_block = (keys, values, token_document_index)
    blocks = [own_block]
    for step in range(1, reach_count + 1):
        blocks.append(passed_along((own_block[0], own_block[1], own_block[2]), "ctx", step))
    query_acc = jnp.zeros((tok_rows, kv_local, q_group, HEAD_WIDTH), jnp.float32)
    pieces = []
    for step in range(reach_count + 1):
        key_block, value_block, seg_block = blocks[step]
        key_heads = key_block.reshape(tok_rows, kv_local, HEAD_WIDTH)
        value_heads = value_block.reshape(tok_rows, kv_local, HEAD_WIDTH)
        scores = (
            jnp.einsum("ikgd,jkd->kgij", query_heads, key_heads, preferred_element_type=jnp.float32)
            * SCORE_SCALE
        )
        distance = offsets[:, None] - offsets[None, :] + step * tok_rows
        allowed = (
            (distance >= 0)
            & (distance < WINDOW)
            & (token_document_index[:, None] == seg_block[None, :])
            & (my_place >= step)
        )
        probs = jnp.where(allowed[None, None], jnp.exp(scores - normalizer[:, :, :, None]), 0.0)
        dprobs = jnp.einsum(
            "ikgd,jkd->kgij", grad_heads, value_heads, preferred_element_type=jnp.float32
        )
        dscore = (probs * (dprobs - row_delta[:, :, :, None])).astype(jnp.bfloat16)
        probs_low = probs.astype(jnp.bfloat16)
        query_acc = query_acc + jnp.einsum(
            "kgij,jkd->ikgd", dscore, key_heads, preferred_element_type=jnp.float32
        )
        key_part = SCORE_SCALE * jnp.einsum(
            "kgij,ikgd->jkd", dscore, query_heads, preferred_element_type=jnp.float32
        )
        value_part = jnp.einsum(
            "kgij,ikgd->jkd", probs_low, grad_heads, preferred_element_type=jnp.float32
        )
        pieces.append(
            (
                key_part.reshape(tok_rows, kv_local * HEAD_WIDTH),
                value_part.reshape(tok_rows, kv_local * HEAD_WIDTH),
            )
        )
    key_sum, value_sum = pieces[0]
    for step in range(1, reach_count + 1):
        moved = passed_along(pieces[step], "ctx", -step)
        key_sum = key_sum + moved[0]
        value_sum = value_sum + moved[1]
    query_gradient_rows = (
        (SCORE_SCALE * query_acc)
        .reshape(tok_rows, kv_local * q_group * HEAD_WIDTH)
        .astype(jnp.bfloat16)
    )
    key_grad = key_sum.astype(jnp.bfloat16)
    value_gradient_rows = value_sum.astype(jnp.bfloat16)
    query_adapter_output = jnp.einsum(
        "zl,ql->zq",
        query_gradient_rows,
        query_adapter_up_weight,
        preferred_element_type=jnp.float32,
    )
    value_adapter_output = jnp.einsum(
        "zl,ql->zq",
        value_gradient_rows,
        value_adapter_up_weight,
        preferred_element_type=jnp.float32,
    )
    query_adapter_input, value_adapter_input = adapter_input_list
    query_backward_rows, value_backward_rows = lax.psum(
        (query_adapter_output, value_adapter_output), "tp"
    )
    query_adapter_input = query_adapter_input.astype(jnp.bfloat16)
    value_adapter_input = value_adapter_input.astype(jnp.bfloat16)
    query_backward_rows = query_backward_rows.astype(jnp.bfloat16)
    value_backward_rows = value_backward_rows.astype(jnp.bfloat16)
    token_scale = 1.0 / math.sqrt(tok_rows * lax.axis_size("ctx"))
    grad_a_query = (
        jnp.einsum(
            "td,tr->dr", layer_input_rows, query_backward_rows, preferred_element_type=jnp.float32
        )
        * token_scale
    )
    grad_b_query = (
        jnp.einsum(
            "tr,tc->rc",
            query_adapter_input,
            query_gradient_rows,
            preferred_element_type=jnp.float32,
        )
        * token_scale
    )
    grad_a_value = (
        jnp.einsum(
            "td,tr->dr", layer_input_rows, value_backward_rows, preferred_element_type=jnp.float32
        )
        * token_scale
    )
    grad_b_value = (
        jnp.einsum(
            "tr,tc->rc",
            value_adapter_input,
            value_gradient_rows,
            preferred_element_type=jnp.float32,
        )
        * token_scale
    )
    summed = lax.psum((grad_a_query, grad_b_query, grad_a_value, grad_b_value), "ctx")
    return (key_grad, summed[0], summed[1], summed[2], summed[3])


def solution(mesh):
    placed = (
        P("ctx", "tp"),
        P("ctx", "tp"),
        P("ctx", "tp"),
        P("ctx", "tp"),
        P("ctx", "tp"),
        P("ctx", "tp"),
        P("tp", "ctx"),
        P("ctx"),
        P("tp", None),
        P(None, "tp"),
        P("tp", None),
        P(None, "tp"),
    )
    return jax.shard_map(
        per_device,
        mesh=mesh,
        in_specs=placed,
        out_specs=(P("ctx", "tp"), P("tp", None), P(None, "tp"), P("tp", None), P(None, "tp")),
        check_vma=False,
    )
```

profile of v0, /device:TPU:1, one launch (start us, length us, event | category | flops | bytes accessed | tf_op | source)
XLA Modules:
  0.0 542.0 jit_solution(7678168712332599871)
XLA Ops:
  7.2 6.2 %collective-permute-start = (s32[1024]{0:T(1024)}, s32[1024]{0:T(1024)S(1)}, u32[]{:S(2)}, u32[]{:S(2)}) collective-permute-start(s32[1024]{0:T(1024)} %param.19), channel_id=1, source_target_pairs={{0,8},{8,16},{16,24},{24,32},{32,40},{40,48},{48,56},{56,64},{64,7... | collective-permute-start | bytes 12296 | tf_op jit(solution)/shard_map/ppermute | solution.py:20
  13.4 3.5 collective-permute-start.4
  16.9 3.5 collective-permute-start.12
  20.5 2.5 collective-permute-start.8
  23.0 4.7 collective-permute-start.6
  28.9 1.5 fusion.189
  30.4 2.3 fusion.191
  33.9 5.7 %fusion.134 = f32[1024,1024,2]{1,0,2:T(8,128)} fusion(bf16[1024,128]{1,0:T(8,128)(2,1)} %param.14, bf16[1024,256]{1,0:T(8,128)(2,1)} %param.13), kind=kOutput, calls=%fused_computation.142 | convolution fusion | flops 536870912 | bytes 9175040 | tf_op jit(solution)/shard_map/ikgd,jkd->kgij/dot_general | solution.py:68
  41.0 6.1 %collective-permute-start.2 = (bf16[1024,128]{1,0:T(8,128)(2,1)}, bf16[1024,128]{1,0:T(8,128)(2,1)}, u32[]{:S(2)}, u32[]{:S(2)}) collective-permute-start(bf16[1024,128]{1,0:T(8,128)(2,1)} %param.15), channel_id=1, source_target_pairs={{0,8},{8,16},{16,24},{24,32},{32,40},{40,48},{48,56},{56,64},{64,7... | collective-permute-start | bytes 786440 | tf_op jit(solution)/shard_map/ppermute | solution.py:20
  47.1 5.5 %collective-permute-start.14 = (bf16[1024,128]{1,0:T(8,128)(2,1)}, bf16[1024,128]{1,0:T(8,128)(2,1)}, u32[]{:S(2)}, u32[]{:S(2)}) collective-permute-start(bf16[1024,128]{1,0:T(8,128)(2,1)} %param.15), channel_id=1, source_target_pairs={{0,32},{8,40},{16,48},{24,56},{32,64},{40,72},{48,80},{56,88},{64,... | collective-permute-start | bytes 786440 | tf_op jit(solution)/shard_map/ppermute | solution.py:20
  52.6 2.0 collective-permute-start.10
  54.6 1.9 collective-permute-start.13
  56.5 8.4 %fusion.73 = (pred[1024,1024]{0,1:T(8,128)(4,1)S(1)}, pred[1024,1024]{0,1:T(8,128)(4,1)}, pred[1024,1024]{0,1:T(8,128)(4,1)S(1)}, pred[1024,1024]{0,1:T(8,128)(4,1)S(1)}, pred[1024,1024]{0,1:T(8,128)(4,1)S(1)}) fusion(s32[1024]{0:T(1024)S(1)} %copy-done.20, pred[]{:T(512)S(6)} %ge.51, pred[]{:T(512)S(6)} %ge.55, s32[1024]{0:T(1024)S(1)} %collective-permute-done.4, ...), kind=kLoop, calls=%fused_computation.79 | loop fusion | flops 36700160 | bytes 5263365 | tf_op jit(solution)/shard_map/and | solution.py:73
  65.0 6.7 %fusion.95 = f32[1024,128]{1,0:T(8,128)} fusion(f32[1024,1024,2]{1,0,2:T(8,128)} %fusion.134, f32[2,1024]{1,0:T(2,128)S(1)} %copy-done.22, pred[1024,1024]{0,1:T(8,128)(4,1)S(1)} %get-tuple-element.13, bf16[1024,256]{1,0:T(8,128)(2,1)} %param.16), kind=kOutput, calls=%fused_computation.95 | convolution fusion | flops 545259520 | bytes 10493952 | tf_op jit(solution)/shard_map/kgij,ikgd->jkd/dot_general | solution.py:90
  72.0 3.1 fusion.30
  75.0 1.9 fusion.151
  77.0 4.1 collective-permute-start.9
  82.3 2.5 fusion.83
  84.8 6.4 %collective-permute-start.5 = (bf16[1024,128]{1,0:T(8,128)(2,1)}, bf16[1024,128]{1,0:T(8,128)(2,1)S(1)}, u32[]{:S(2)}, u32[]{:S(2)}) collective-permute-start(bf16[1024,128]{1,0:T(8,128)(2,1)} %param.14), channel_id=1, source_target_pairs={{0,16},{8,24},{16,32},{24,40},{32,48},{40,56},{48,64},{56,72},{64,... | collective-permute-start | bytes 786440 | tf_op jit(solution)/shard_map/ppermute | solution.py:20
  92.5 2.5 fusion.86
  94.9 2.4 collective-permute-start.1
  97.3 4.1 fusion.34
  101.4 2.1 fusion.98
  106.0 2.5 fusion.92
  108.5 1.5 collective-permute-start.19
  110.0 4.4 fusion.33
  114.4 2.2 fusion.99
  117.9 4.4 fusion.31
  122.3 2.1 fusion.101
  124.4 1.9 collective-permute-start.16
  127.7 1.7 fusion.89
  130.9 1.5 collective-permute-start.17
  132.5 4.0 fusion.32
  139.3 2.1 fusion.100
  143.8 1.9 collective-permute-start.3
  147.0 1.9 collective-permute-done.17
  149.0 1.3 add_convert_fusion
  151.3 86.8 %all-reduce.6 = (bf16[1024,128]{1,0:T(8,128)(2,1)}, bf16[1024,128]{1,0:T(8,128)(2,1)}, bf16[1024,128]{1,0:T(8,128)(2,1)}, bf16[1024,128]{1,0:T(8,128)(2,1)}) all-reduce(f32[1024,128]{1,0:T(8,128)} %fusion.188, f32[1024,128]{1,0:T(8,128)S(1)} %fusion.189, f32[1024,128]{1,0:T(8,128)} %fusion.190, ...), channel_id=1, replica_groups=mesh['ctx'=32,'tp'=8] {'tp'}, use_global_device_ids=true, to_apply=%region_0.0 | all-reduce | flops 524288 | bytes 3145728 | tf_op jit(solution)/shard_map/psum | solution.py:124
  238.1 1.9 convolution_multiply_fusion.2
  240.0 2.1 fusion.108
  242.2 2.1 fusion.109
  244.3 1.8 convolution_multiply_fusion.3
  246.2 4.7 fusion.107
  250.9 277.4 %all-reduce.5.cloned.1.call-done = (f32[576,128]{1,0:T(8,128)}, f32[128,256]{1,0:T(8,128)}, f32[576,128]{1,0:T(8,128)}, f32[128,128]{1,0:T(8,128)}) async-done(((f32[576,128]{1,0:T(8,128)}, f32[128,256]{1,0:T(8,128)}, f32[576,128]{1,0:T(8,128)}, f32[128,128]{1,0:T(8,128)}), (f32[576,128]{1,0:T(8,128)}, f32[128,256]{1,0:T(8,128)}, f32[576,128]{1,0:T(8,128)}, ...) | async-done | bytes 786448 | tf_op jit(solution)/shard_map/psum | solution.py:162
  528.3 1.7 copy.164
  530.0 1.6 copy.165
  531.6 1.7 copy.166
  533.3 1.5 copy.167
  (90 shorter events, 20.7 us)
Async XLA Ops:
  7.2 21.7 %copy-start = (bf16[1024,576]{0,1:T(8,128)(2,1)S(1)}, bf16[1024,576]{0,1:T(8,128)(2,1)}, u32[]{:S(2)}) copy-start(bf16[1024,576]{0,1:T(8,128)(2,1)} %param.12) | copy-start | bytes 3538948
  7.2 49.3 %copy-start.20 = (s32[1024]{0:T(1024)S(1)}, s32[1024]{0:T(1024)}, u32[]{:S(2)}) copy-start(s32[1024]{0:T(1024)} %param.19) | copy-start | bytes 12292
  7.2 521.1 %all-reduce.5.cloned.1.call-start = ((), (), s32[]{:S(2)}) async-start(), calls=%async_computation | async-start | bytes 1572864 | tf_op jit(solution)/shard_map/psum | solution.py:162
  7.2 33.8 %collective-permute-start = (s32[1024]{0:T(1024)}, s32[1024]{0:T(1024)S(1)}, u32[]{:S(2)}, u32[]{:S(2)}) collective-permute-start(s32[1024]{0:T(1024)} %param.19), channel_id=1, source_target_pairs={{0,8},{8,16},{16,24},{24,32},{32,40},{40,48},{48,56},{56,64},{64,7... | collective-permute-start | bytes 12296 | tf_op jit(solution)/shard_map/ppermute | solution.py:20
  13.4 33.7 %collective-permute-start.4 = (s32[1024]{0:T(1024)}, s32[1024]{0:T(1024)S(1)}, u32[]{:S(2)}, u32[]{:S(2)}) collective-permute-start(s32[1024]{0:T(1024)} %param.19), channel_id=1, source_target_pairs={{0,16},{8,24},{16,32},{24,40},{32,48},{40,56},{48,64},{56,72},{64,... | collective-permute-start | bytes 12296 | tf_op jit(solution)/shard_map/ppermute | solution.py:20
  16.9 35.7 %collective-permute-start.12 = (s32[1024]{0:T(1024)}, s32[1024]{0:T(1024)S(1)}, u32[]{:S(2)}, u32[]{:S(2)}) collective-permute-start(s32[1024]{0:T(1024)} %param.19), channel_id=1, source_target_pairs={{0,32},{8,40},{16,48},{24,56},{32,64},{40,72},{48,80},{56,88},{64,... | collective-permute-start | bytes 12296 | tf_op jit(solution)/shard_map/ppermute | solution.py:20
  20.5 34.1 %collective-permute-start.8 = (s32[1024]{0:T(1024)}, s32[1024]{0:T(1024)S(1)}, u32[]{:S(2)}, u32[]{:S(2)}) collective-permute-start(s32[1024]{0:T(1024)} %param.19), channel_id=1, source_target_pairs={{0,24},{8,32},{16,40},{24,48},{32,56},{40,64},{48,72},{56,80},{64,... | collective-permute-start | bytes 12296 | tf_op jit(solution)/shard_map/ppermute | solution.py:20
  23.0 107.9 %collective-permute-start.6 = (bf16[1024,128]{1,0:T(8,128)(2,1)}, bf16[1024,128]{1,0:T(8,128)(2,1)}, u32[]{:S(2)}, u32[]{:S(2)}) collective-permute-start(bf16[1024,128]{1,0:T(8,128)(2,1)} %param.15), channel_id=1, source_target_pairs={{0,16},{8,24},{16,32},{24,40},{32,48},{40,56},{48,64},{56,72},{64,... | collective-permute-start | bytes 786440 | tf_op jit(solution)/shard_map/ppermute | solution.py:20
  33.9 31.1 %copy-start.22 = (f32[2,1024]{1,0:T(2,128)S(1)}, f32[2,1024]{1,0:T(2,128)}, u32[]{:S(2)}) copy-start(f32[2,1024]{1,0:T(2,128)} %param.18) | copy-start | bytes 24580
  41.0 75.6 %collective-permute-start.2 = (bf16[1024,128]{1,0:T(8,128)(2,1)}, bf16[1024,128]{1,0:T(8,128)(2,1)}, u32[]{:S(2)}, u32[]{:S(2)}) collective-permute-start(bf16[1024,128]{1,0:T(8,128)(2,1)} %param.15), channel_id=1, source_target_pairs={{0,8},{8,16},{16,24},{24,32},{32,40},{40,48},{48,56},{56,64},{64,7... | collective-permute-start | bytes 786440 | tf_op jit(solution)/shard_map/ppermute | solution.py:20
  47.1 47.8 %collective-permute-start.14 = (bf16[1024,128]{1,0:T(8,128)(2,1)}, bf16[1024,128]{1,0:T(8,128)(2,1)}, u32[]{:S(2)}, u32[]{:S(2)}) collective-permute-start(bf16[1024,128]{1,0:T(8,128)(2,1)} %param.15), channel_id=1, source_target_pairs={{0,32},{8,40},{16,48},{24,56},{32,64},{40,72},{48,80},{56,88},{64,... | collective-permute-start | bytes 786440 | tf_op jit(solution)/shard_map/ppermute | solution.py:20
  52.6 56.0 %collective-permute-start.10 = (bf16[1024,128]{1,0:T(8,128)(2,1)}, bf16[1024,128]{1,0:T(8,128)(2,1)}, u32[]{:S(2)}, u32[]{:S(2)}) collective-permute-start(bf16[1024,128]{1,0:T(8,128)(2,1)} %param.15), channel_id=1, source_target_pairs={{0,24},{8,32},{16,40},{24,48},{32,56},{40,64},{48,72},{56,80},{64,... | collective-permute-start | bytes 786440 | tf_op jit(solution)/shard_map/ppermute | solution.py:20
  54.6 22.4 %collective-permute-start.13 = (bf16[1024,128]{1,0:T(8,128)(2,1)}, bf16[1024,128]{1,0:T(8,128)(2,1)S(1)}, u32[]{:S(2)}, u32[]{:S(2)}) collective-permute-start(bf16[1024,128]{1,0:T(8,128)(2,1)} %param.14), channel_id=1, source_target_pairs={{0,32},{8,40},{16,48},{24,56},{32,64},{40,72},{48,80},{56,88},{64,... | collective-permute-start | bytes 786440 | tf_op jit(solution)/shard_map/ppermute | solution.py:20
  64.9 27.5 %copy-start.8 = (pred[1024,1024]{0,1:T(8,128)(4,1)}, pred[1024,1024]{0,1:T(8,128)(4,1)S(1)}, u32[]{:S(2)}) copy-start(pred[1024,1024]{0,1:T(8,128)(4,1)S(1)} %get-tuple-element.15) | copy-start | bytes 3145732
  64.9 41.1 %copy-start.7 = (pred[1024,1024]{0,1:T(8,128)(4,1)}, pred[1024,1024]{0,1:T(8,128)(4,1)S(1)}, u32[]{:S(2)}) copy-start(pred[1024,1024]{0,1:T(8,128)(4,1)S(1)} %get-tuple-element.17) | copy-start | bytes 3145732
  65.0 6.8 %slice-start = ((s8[8388608]{0:T(1024)(128)(4,1)}), s8[4194304]{0:T(1024)(128)(4,1)S(1)}, s32[]{:S(2)}) async-start(s8[8388608]{0:T(1024)(128)(4,1)} %bitcast.410), calls=%async_computation.1 | async-start | bytes 8388608
  65.0 6.8 %copy-start.15 = (bf16[1024,256]{1,0:T(8,128)(2,1)S(1)}, bf16[1024,256]{1,0:T(8,128)(2,1)}, u32[]{:S(2)}) copy-start(bf16[1024,256]{1,0:T(8,128)(2,1)} %param.16) | copy-start | bytes 1572868
  65.0 6.8 %copy-start.21 = (bf16[1024,128]{1,0:T(8,128)(2,1)S(1)}, bf16[1024,128]{1,0:T(8,128)(2,1)}, u32[]{:S(2)}) copy-start(bf16[1024,128]{1,0:T(8,128)(2,1)} %param.15) | copy-start | bytes 786436
  65.0 7.0 %slice-start.1 = ((s8[8388608]{0:T(1024)(128)(4,1)}), s8[4194304]{0:T(1024)(128)(4,1)S(1)}, s32[]{:S(2)}) async-start(s8[8388608]{0:T(1024)(128)(4,1)} %bitcast.410), calls=%async_computation.2 | async-start | bytes 8388608
  72.0 9.1 %copy-start.2 = (bf16[1024,256]{1,0:T(8,128)(2,1)S(1)}, bf16[1024,256]{1,0:T(8,128)(2,1)}, u32[]{:S(2)}) copy-start(bf16[1024,256]{1,0:T(8,128)(2,1)} %param.13) | copy-start | bytes 1572868
  75.0 9.7 %copy-start.1 = (bf16[2,1024,1024]{1,2,0:T(8,128)(2,1)}, bf16[2,1024,1024]{1,2,0:T(8,128)(2,1)S(1)}, u32[]{:S(2)}) copy-start(bf16[2,1024,1024]{1,2,0:T(8,128)(2,1)S(1)} %fusion.30) | copy-start | bytes 12582916
  77.0 7.8 %copy-start.11 = (bf16[1024,128]{1,0:T(8,128)(2,1)}, bf16[1024,128]{1,0:T(8,128)(2,1)S(1)}, u32[]{:S(2)}) copy-start(bf16[1024,128]{1,0:T(8,128)(2,1)S(1)} %collective-permute-done.13) | copy-start | bytes 786436
  77.0 7.8 %collective-permute-start.9 = (bf16[1024,128]{1,0:T(8,128)(2,1)}, bf16[1024,128]{1,0:T(8,128)(2,1)S(1)}, u32[]{:S(2)}, u32[]{:S(2)}) collective-permute-start(bf16[1024,128]{1,0:T(8,128)(2,1)} %param.14), channel_id=1, source_target_pairs={{0,24},{8,32},{16,40},{24,48},{32,56},{40,64},{48,72},{56,80},{64,... | collective-permute-start | bytes 786440 | tf_op jit(solution)/shard_map/ppermute | solution.py:20
  84.8 10.2 %copy-start.13 = (bf16[1024,128]{1,0:T(8,128)(2,1)}, bf16[1024,128]{1,0:T(8,128)(2,1)S(1)}, u32[]{:S(2)}) copy-start(bf16[1024,128]{1,0:T(8,128)(2,1)S(1)} %collective-permute-done.9) | copy-start | bytes 786436
  84.8 39.6 %collective-permute-start.5 = (bf16[1024,128]{1,0:T(8,128)(2,1)}, bf16[1024,128]{1,0:T(8,128)(2,1)S(1)}, u32[]{:S(2)}, u32[]{:S(2)}) collective-permute-start(bf16[1024,128]{1,0:T(8,128)(2,1)} %param.14), channel_id=1, source_target_pairs={{0,16},{8,24},{16,32},{24,40},{32,48},{40,56},{48,64},{56,72},{64,... | collective-permute-start | bytes 786440 | tf_op jit(solution)/shard_map/ppermute | solution.py:20
  94.9 8.5 %collective-permute-start.1 = (bf16[1024,128]{1,0:T(8,128)(2,1)}, bf16[1024,128]{1,0:T(8,128)(2,1)S(1)}, u32[]{:S(2)}, u32[]{:S(2)}) collective-permute-start(bf16[1024,128]{1,0:T(8,128)(2,1)} %param.14), channel_id=1, source_target_pairs={{0,8},{8,16},{16,24},{24,32},{32,40},{40,48},{48,56},{56,64},{64,7... | collective-permute-start | bytes 786440 | tf_op jit(solution)/shard_map/ppermute | solution.py:20
  103.5 5.1 copy-start.9
  103.5 142.7 %collective-permute-start.15 = (f32[1024,128]{1,0:T(8,128)}, f32[1024,128]{1,0:T(8,128)}, u32[]{:S(2)}, u32[]{:S(2)}) collective-permute-start(f32[1024,128]{1,0:T(8,128)} %fusion.98), channel_id=1, source_target_pairs={{32,0},{40,8},{48,16},{56,24},{64,32},{72,40},{80,48},{88,56},{96,... | collective-permute-start | bytes 1572872 | tf_op jit(solution)/shard_map/ppermute | solution.py:20
  108.5 32.9 %collective-permute-start.19 = (f32[1024,128]{1,0:T(8,128)}, f32[1024,128]{1,0:T(8,128)}, u32[]{:S(2)}, u32[]{:S(2)}) collective-permute-start(f32[1024,128]{1,0:T(8,128)} %fusion.83), channel_id=1, source_target_pairs={{32,0},{40,8},{48,16},{56,24},{64,32},{72,40},{80,48},{88,56},{96,... | collective-permute-start | bytes 1572872 | tf_op jit(solution)/shard_map/ppermute | solution.py:20
  114.4 2.2 copy-start.3
  116.6 27.2 %collective-permute-start.18 = (f32[1024,128]{1,0:T(8,128)}, f32[1024,128]{1,0:T(8,128)}, u32[]{:S(2)}, u32[]{:S(2)}) collective-permute-start(f32[1024,128]{1,0:T(8,128)} %fusion.86), channel_id=1, source_target_pairs={{24,0},{32,8},{40,16},{48,24},{56,32},{64,40},{72,48},{80,56},{88,... | collective-permute-start | bytes 1572872 | tf_op jit(solution)/shard_map/ppermute | solution.py:20
  122.3 5.3 copy-start.6
  122.3 5.3 copy-start.16
  124.4 21.3 %collective-permute-start.16 = (f32[1024,128]{1,0:T(8,128)}, f32[1024,128]{1,0:T(8,128)S(1)}, u32[]{:S(2)}, u32[]{:S(2)}) collective-permute-start(f32[1024,128]{1,0:T(8,128)} %fusion.92), channel_id=1, source_target_pairs={{8,0},{16,8},{24,16},{32,24},{40,32},{48,40},{56,48},{64,56},{72,6... | collective-permute-start | bytes 1572872 | tf_op jit(solution)/shard_map/ppermute | solution.py:20
  127.6 1.7 copy-start.12
  127.6 2.5 copy-start.4
  127.6 2.5 copy-start.14
  130.9 5.6 %copy-start.10 = (bf16[1024,128]{1,0:T(8,128)(2,1)S(1)}, bf16[1024,128]{1,0:T(8,128)(2,1)}, u32[]{:S(2)}) copy-start(bf16[1024,128]{1,0:T(8,128)(2,1)} %copy-done.9) | copy-start | bytes 786436
  130.9 18.0 %collective-permute-start.17 = (f32[1024,128]{1,0:T(8,128)S(1)}, f32[1024,128]{1,0:T(8,128)S(1)}, u32[]{:S(2)}, u32[]{:S(2)}) collective-permute-start(f32[1024,128]{1,0:T(8,128)S(1)} %fusion.89), channel_id=1, source_target_pairs={{16,0},{24,8},{32,16},{40,24},{48,32},{56,40},{64,48},{72,56},{80,... | collective-permute-start | bytes 1572872 | tf_op jit(solution)/shard_map/ppermute | solution.py:20
  136.5 1.7 copy-start.18
  137.3 11.6 %copy-start.17 = (f32[1024,128]{1,0:T(8,128)S(1)}, f32[1024,128]{1,0:T(8,128)}, u32[]{:S(2)}) copy-start(f32[1024,128]{1,0:T(8,128)} %fusion.95) | copy-start | bytes 1572868
  137.3 13.0 %copy-start.19 = (bf16[128,128]{1,0:T(8,128)(2,1)S(1)}, bf16[128,128]{1,0:T(8,128)(2,1)}, u32[]{:S(2)}) copy-start(bf16[128,128]{1,0:T(8,128)(2,1)} %param.23) | copy-start | bytes 98308
  137.3 14.0 %copy-start.5 = (f32[1024,128]{1,0:T(8,128)S(1)}, f32[1024,128]{1,0:T(8,128)}, u32[]{:S(2)}) copy-start(f32[1024,128]{1,0:T(8,128)} %fusion.191) | copy-start | bytes 1572868
  141.4 104.8 %collective-permute-start.11 = (f32[1024,128]{1,0:T(8,128)}, f32[1024,128]{1,0:T(8,128)}, u32[]{:S(2)}, u32[]{:S(2)}) collective-permute-start(f32[1024,128]{1,0:T(8,128)} %fusion.99), channel_id=1, source_target_pairs={{24,0},{32,8},{40,16},{48,24},{56,32},{64,40},{72,48},{80,56},{88,... | collective-permute-start | bytes 1572872 | tf_op jit(solution)/shard_map/ppermute | solution.py:20
  143.8 102.4 %collective-permute-start.3 = (f32[1024,128]{1,0:T(8,128)}, f32[1024,128]{1,0:T(8,128)}, u32[]{:S(2)}, u32[]{:S(2)}) collective-permute-start(f32[1024,128]{1,0:T(8,128)} %fusion.101), channel_id=1, source_target_pairs={{8,0},{16,8},{24,16},{32,24},{40,32},{48,40},{56,48},{64,56},{72,6... | collective-permute-start | bytes 1572872 | tf_op jit(solution)/shard_map/ppermute | solution.py:20
  145.7 100.5 %collective-permute-start.7 = (f32[1024,128]{1,0:T(8,128)}, f32[1024,128]{1,0:T(8,128)}, u32[]{:S(2)}, u32[]{:S(2)}) collective-permute-start(f32[1024,128]{1,0:T(8,128)} %fusion.100), channel_id=1, source_target_pairs={{16,0},{24,8},{32,16},{40,24},{48,32},{56,40},{64,48},{72,56},{80,... | collective-permute-start | bytes 1572872 | tf_op jit(solution)/shard_map/ppermute | solution.py:20
Sparse Core Ops, SparseCore 0:
  246.3 281.9 all-reduce.4
where the time goes:
time: 550 us; the launch traced here: 542 us
  waiting for transfers between devices  280 us (51%)
  blocking collectives  86.8 us (16%)
  matrix products  78.5 us (14%)
  starting transfers between devices  60.9 us (11%)
  between operations  15.1 us (3%)
  other arithmetic  11 us (2%)
  local copies, waits for them, and re-layouts  9.28 us (2%)
    psum x1, waiting for transfers between devices, per_device(): lax.psum((grad_a_query, grad_b_query, grad_a_value, grad_b_value), 'ctx')  277 us
    psum x1, blocking collectives, per_device(): lax.psum((query_adapter_output, value_adapter_output), 'tp')  86.8 us
    ppermute x20, starting transfers between devices, passed_along(): lax.ppermute(value, axis, [(source, source + steps) for source in range(f...  60.8 us
    dot_general x5, matrix products, per_device(): jnp.einsum('ikgd,jkd->kgij', grad_heads, value_heads, preferred_element_t...  19.9 us
    dot_general x5, matrix products, per_device(): jnp.einsum('kgij,ikgd->jkd', probs_low, grad_heads, preferred_element_typ...  15.8 us
    dot_general x5, matrix products, per_device(): jnp.einsum('kgij,ikgd->jkd', dscore, query_heads, preferred_element_type=...  13.1 us
  transfers between devices with their start and end apart: 21, of which 3 were waited for; matrix products, arithmetic and copies ran while one was open for 17% of the time, Pallas kernels for 0%

commit v1 on v0

v1 whole, which is shorter than its diff:
```python
import functools
import math

import jax
import jax.numpy as jnp
from jax import lax
from jax.experimental import pallas as pl
from jax.experimental.pallas import tpu as pltpu
from jax.sharding import PartitionSpec as P

HEAD = 128
HEADS_LOCAL = 2
REACH = 4
SCORE_SCALE = 144.0 ** (-0.5)
LOG2E = 1.4426950408889634
BF16 = jnp.bfloat16
F32 = jnp.float32
MESH = pl.DeviceIdType.MESH


def contract(a, b, dim_a, dim_b):
    return lax.dot_general(
        a, b, (((dim_a,), (dim_b,)), ((), ())), preferred_element_type=F32
    )


def kernel(
    n_ctx,
    n_tp,
    x_ref,
    q_ref,
    k_ref,
    v_ref,
    do_ref,
    o_ref,
    lse_ref,
    seg_ref,
    aq_ref,
    bq_ref,
    av_ref,
    bv_ref,
    key_grad_ref,
    ga_q_ref,
    gb_q_ref,
    ga_v_ref,
    gb_v_ref,
    k_in,
    v_in,
    seg_in,
    q_st,
    do_st,
    lse_st,
    delta_st,
    thr_st,
    dk_acc,
    dv_acc,
    dk_own,
    dv_own,
    dq_acc,
    dq_low,
    dv_low,
    part_out,
    part_in,
    low_s,
    low_r,
    low_g,
    back_s,
    back_r,
    back_g,
    g_all,
    half_s,
    half_r,
    piece_s,
    piece_r,
    g_out,
    kv_send,
    kv_recv,
    part_send,
    part_recv,
    tp_send,
    tp_recv,
    half_send,
    half_recv,
    piece_send,
    piece_recv,
):
    rows = k_ref.shape[0]
    width = x_ref.shape[1]
    chunk = rows // n_tp
    pairs = n_ctx // 2
    total = g_all.shape[0]
    half = total // 2
    piece = half // pairs
    c = lax.axis_index("ctx")
    t = lax.axis_index("tp")
    core = lax.rem(c, 2)
    pair = c // 2

    def ctx_at(offset):
        return lax.rem(c + (offset + n_ctx), n_ctx)

    def tp_at(offset):
        return lax.rem(t + offset, n_tp)

    barrier = pltpu.get_barrier_semaphore()
    offsets = {s % n_ctx for s in range(-REACH, REACH + 1)} | set(range(0, n_ctx, 2))
    offsets = sorted(offsets - {0})
    for offset in offsets:
        pl.semaphore_signal(
            barrier, inc=1, device_id={"ctx": ctx_at(offset)}, device_id_type=MESH
        )
    for offset in range(1, n_tp):
        pl.semaphore_signal(
            barrier, inc=1, device_id={"tp": tp_at(offset)}, device_id_type=MESH
        )
    pl.semaphore_wait(barrier, len(offsets) + n_tp - 1)

    def kv_copies(step):
        found = []
        for which, (src, dst) in enumerate(
            ((k_ref, k_in), (v_ref, v_in), (seg_ref, seg_in))
        ):
            found.append(
                pltpu.make_async_remote_copy(
                    src_ref=src,
                    dst_ref=dst.at[step - 1],
                    send_sem=kv_send.at[which, step - 1],
                    recv_sem=kv_recv.at[which, step - 1],
                    device_id={"ctx": ctx_at(step)},
                    device_id_type=MESH,
                )
            )
        return found

    for step in range(1, REACH + 1):
        for copy in kv_copies(step):
            copy.start()

    def part_copy(step):
        return pltpu.make_async_remote_copy(
            src_ref=part_out.at[step - 1],
            dst_ref=part_in.at[step - 1],
            send_sem=part_send.at[step - 1],
            recv_sem=part_recv.at[step - 1],
            device_id={"ctx": ctx_at(-step)},
            device_id_type=MESH,
        )

    def scatter_copy(which, src, dst, first, high, offset):
        to = tp_at(offset)
        return pltpu.make_async_remote_copy(
            src_ref=src.at[pl.ds(first, high), pl.ds(pl.multiple_of(to * chunk, chunk), chunk)],
            dst_ref=dst.at[offset, pl.ds(first, high)],
            send_sem=tp_send.at[which, offset],
            recv_sem=tp_recv.at[which, offset],
            device_id={"tp": to},
            device_id_type=MESH,
        )

    mine = pl.ds(pl.multiple_of(t * chunk, chunk), chunk)

    def gather_copy(which, ref, first, high, offset):
        place = ref.at[pl.ds(first, high), mine]
        return pltpu.make_async_remote_copy(
            src_ref=place,
            dst_ref=place,
            send_sem=tp_send.at[which, offset],
            recv_sem=tp_recv.at[which, offset],
            device_id={"tp": tp_at(offset)},
            device_id_type=MESH,
        )

    def scatter_start(which, src, dst, first, high):
        for offset in range(1, n_tp):
            scatter_copy(which, src, dst, first, high, offset).start()

    def scatter_finish(which, src, dst, ref, first, high):
        for offset in range(1, n_tp):
            scatter_copy(which, src, dst, first, high, offset).wait()
        part = src[first : first + high, mine].astype(F32)
        for offset in range(1, n_tp):
            part = part + dst[offset, first : first + high, :].astype(F32)
        ref[first : first + high, mine] = part.astype(BF16)
        for offset in range(1, n_tp):
            gather_copy(which + 1, ref, first, high, offset).start()

    def gather_finish(which, ref, first, high):
        for offset in range(1, n_tp):
            gather_copy(which + 1, ref, first, high, offset).wait()

    low_s[0:HEAD, :] = contract(aq_ref[...], x_ref[...], 0, 1).astype(BF16)
    low_s[HEAD : 2 * HEAD, :] = contract(av_ref[...], x_ref[...], 0, 1).astype(BF16)
    scatter_start(0, low_s, low_r, 0, 2 * HEAD)

    ones = jnp.ones((8, HEAD), BF16)
    for h in range(HEADS_LOCAL):
        cols = slice(h * HEAD, (h + 1) * HEAD)
        span = slice(h * rows, (h + 1) * rows)
        q_st[span, :] = q_ref[:, cols]
        grad = do_ref[:, cols]
        do_st[span, :] = grad
        prod = grad.astype(F32) * o_ref[:, cols].astype(F32)
        high = prod.astype(BF16)
        rest = (prod - high.astype(F32)).astype(BF16)
        delta = contract(ones, high, 1, 1) + contract(ones, rest, 1, 1)
        delta_st[:, span] = delta[0:1, :]
        lse_st[:, span] = lse_ref[h : h + 1, :] * LOG2E

    def first_allowed(block, present):
        ids = seg_ref[...]
        found = jnp.zeros((1, rows), jnp.int32)
        for doc in range(1, 4):
            below = jnp.sum((block < doc).astype(F32), axis=1, keepdims=True)
            found = jnp.where(ids == doc, below.astype(jnp.int32), found)
        return jnp.where(present, found, rows)

    def set_thr(found):
        for h in range(HEADS_LOCAL):
            thr_st[:, h * rows : (h + 1) * rows] = found

    def tile(keys, values, sum_k, sum_v, k0, kt, r0, rt, causal):
        ks, rs = slice(k0, k0 + kt), slice(r0, r0 + rt)
        key, value = keys[ks, :], values[ks, :]
        query, grad = q_st[rs, :], do_st[rs, :]
        j = lax.broadcasted_iota(jnp.int32, (kt, rt), 0) + k0
        mask = j >= thr_st[:, rs]
        if causal:
            i = lax.broadcasted_iota(jnp.int32, (1, rt), 1) + (r0 % rows)
            mask = mask & (j <= i)
        score = contract(key, query, 1, 1)
        dprob = contract(value, grad, 1, 1)
        prob = jnp.where(mask, jnp.exp2(score * (SCORE_SCALE * LOG2E) - lse_st[:, rs]), 0.0)
        dscore = (prob * (dprob - delta_st[:, rs])).astype(BF16)
        sum_v[ks, :] += contract(prob.astype(BF16), grad, 1, 0)
        sum_k[ks, :] += contract(dscore, query, 1, 0)
        dq_acc[:, rs] += contract(key, dscore, 0, 0)

    edge = min(256, rows)
    wide = min(512, rows)

    dq_acc[...] = jnp.zeros_like(dq_acc)
    dk_own[...] = jnp.zeros_like(dk_own)
    dv_own[...] = jnp.zeros_like(dv_own)
    set_thr(first_allowed(seg_ref[...], True))
    for h in range(HEADS_LOCAL):
        for r in range(0, rows, edge):
            if r:
                tile(k_ref, v_ref, dk_own, dv_own, 0, r, h * rows + r, edge, False)
            tile(k_ref, v_ref, dk_own, dv_own, r, edge, h * rows + r, edge, True)

    scatter_finish(0, low_s, low_r, low_g, 0, 2 * HEAD)

    def open_step(step):
        for copy in kv_copies(step):
            copy.wait()
        dk_acc[...] = jnp.zeros_like(dk_acc)
        dv_acc[...] = jnp.zeros_like(dv_acc)
        return first_allowed(seg_in[step - 1], c >= step)

    def close_step(step):
        part_out[step - 1, 0] = (SCORE_SCALE * dk_acc[...]).astype(BF16)
        part_out[step - 1, 1] = dv_acc[...].astype(BF16)
        part_copy(step).start()

    def full_step(step, carry):
        set_thr(open_step(step))
        keys, values = k_in.at[step - 1], v_in.at[step - 1]
        for r in range(0, HEADS_LOCAL * rows, wide):
            for k0 in range(0, rows, wide):
                tile(keys, values, dk_acc, dv_acc, k0, wide, r, wide, False)
        close_step(step)
        return carry

    lax.fori_loop(1, REACH, full_step, 0)

    i = lax.broadcasted_iota(jnp.int32, (1, rows), 1)
    set_thr(jnp.maximum(open_step(REACH), i + 1))
    for h in range(HEADS_LOCAL):
        for r in range(0, rows, edge):
            tile(
                k_in.at[REACH - 1], v_in.at[REACH - 1], dk_acc, dv_acc,
                r, rows - r, h * rows + r, edge, False,
            )
    close_step(REACH)

    token_scale = 1.0 / math.sqrt(rows * n_ctx)

    dq_low[...] = (SCORE_SCALE * dq_acc[...]).astype(BF16)
    back_s[0:HEAD, :] = (
        contract(bq_ref[:, 0:HEAD], dq_low[:, 0:rows], 1, 0)
        + contract(bq_ref[:, HEAD : 2 * HEAD], dq_low[:, rows : 2 * rows], 1, 0)
    ).astype(BF16)
    scatter_start(2, back_s, back_r, 0, HEAD)
    gather_finish(0, low_g, 0, 2 * HEAD)
    base = 2 * width
    for h in range(HEADS_LOCAL):
        g_all[base + h * HEAD : base + (h + 1) * HEAD, :] = token_scale * contract(
            dq_low[:, h * rows : (h + 1) * rows], low_g[0:HEAD, :], 1, 1
        )
    scatter_finish(2, back_s, back_r, back_g, 0, HEAD)

    dk_sum = SCORE_SCALE * dk_own[...]
    dv_sum = dv_own[...]
    for step in range(1, REACH + 1):
        part_copy(step).wait()
        dv_sum = dv_sum + part_in[step - 1, 1].astype(F32)
    dv_low[...] = dv_sum.astype(BF16)
    back_s[HEAD : 2 * HEAD, :] = contract(bv_ref[...], dv_low[...], 1, 1).astype(BF16)
    scatter_start(4, back_s, back_r, HEAD, HEAD)
    for step in range(1, REACH + 1):
        dk_sum = dk_sum + part_in[step - 1, 0].astype(F32)
    key_grad_ref[...] = dk_sum.astype(BF16)
    g_all[total - HEAD : total, :] = token_scale * contract(
        low_g[HEAD : 2 * HEAD, :], dv_low[...], 1, 0
    )
    gather_finish(2, back_g, 0, HEAD)
    g_all[0:width, :] = token_scale * contract(back_g[0:HEAD, :], x_ref[...], 1, 0).T
    scatter_finish(4, back_s, back_r, back_g, HEAD, HEAD)
    gather_finish(4, back_g, HEAD, HEAD)
    g_all[width : 2 * width, :] = (
        token_scale * contract(back_g[HEAD : 2 * HEAD, :], x_ref[...], 1, 0).T
    )

    other = 1 - core
    own_half = pl.ds(pl.multiple_of(core * half, 16), half)
    half_s[...] = g_all[pl.ds(pl.multiple_of(other * half, 16), half), :].astype(BF16)

    def to_other(which, src, dst):
        return pltpu.make_async_remote_copy(
            src_ref=src,
            dst_ref=dst,
            send_sem=half_send.at[which],
            recv_sem=half_recv.at[which],
            device_id={"ctx": c + other - core},
            device_id_type=MESH,
        )

    swap = to_other(0, half_s, half_r)
    swap.start()
    swap.wait()
    g_all[0:half, :] = g_all[own_half, :] + half_r[...].astype(F32)
    piece_s[...] = g_all[0:half, :].astype(BF16)

    def piece_copy(offset):
        to = lax.rem(pair + offset, pairs)
        return pltpu.make_async_remote_copy(
            src_ref=piece_s.at[pl.ds(pl.multiple_of(to * piece, 16), piece)],
            dst_ref=piece_r.at[offset],
            send_sem=piece_send.at[0, offset],
            recv_sem=piece_recv.at[0, offset],
            device_id={"ctx": 2 * to + core},
            device_id_type=MESH,
        )

    for offset in range(1, pairs):
        piece_copy(offset).start()
    summed = g_all[pl.ds(pl.multiple_of(pair * piece, 16), piece), :]
    for offset in range(1, pairs):
        piece_copy(offset).wait()
        summed = summed + piece_r[offset].astype(F32)
    own_piece = pl.ds(pl.multiple_of(core * half + pair * piece, 16), piece)
    g_out[own_piece, :] = summed.astype(BF16)

    def spread_copy(offset):
        to = lax.rem(pair + offset, pairs)
        return pltpu.make_async_remote_copy(
            src_ref=g_out.at[own_piece],
            dst_ref=g_out.at[own_piece],
            send_sem=piece_send.at[1, offset],
            recv_sem=piece_recv.at[1, offset],
            device_id={"ctx": 2 * to + core},
            device_id_type=MESH,
        )

    for offset in range(1, pairs):
        spread_copy(offset).start()
    for offset in range(1, pairs):
        spread_copy(offset).wait()
    swap = to_other(1, g_out.at[own_half], g_out.at[own_half])
    swap.start()
    swap.wait()

    ga_q_ref[...] = g_out[0:width, :].astype(F32)
    ga_v_ref[...] = g_out[width : 2 * width, :].astype(F32)
    for h in range(HEADS_LOCAL):
        gb_q_ref[:, h * HEAD : (h + 1) * HEAD] = (
            g_out[base + h * HEAD : base + (h + 1) * HEAD, :].astype(F32).T
        )
    gb_v_ref[...] = g_out[total - HEAD : total, :].astype(F32)


def per_device(x, q, k, v, do, o, lse, seg, aq, bq, av, bv):
    n_ctx, n_tp = lax.axis_size("ctx"), lax.axis_size("tp")
    rows, width = x.shape
    chunk = rows // n_tp
    total = 2 * width + 3 * HEAD
    half = total // 2
    pairs = n_ctx // 2
    piece = half // pairs
    dma = pltpu.SemaphoreType.DMA
    vmem = pltpu.VMEM
    scratch = [
        vmem((REACH, rows, HEAD), BF16),
        vmem((REACH, rows, HEAD), BF16),
        vmem((REACH, 1, rows), jnp.int32),
        vmem((2 * rows, HEAD), BF16),
        vmem((2 * rows, HEAD), BF16),
        vmem((1, 2 * rows), F32),
        vmem((1, 2 * rows), F32),
        vmem((1, 2 * rows), jnp.int32),
        vmem((rows, HEAD), F32),
        vmem((rows, HEAD), F32),
        vmem((rows, HEAD), F32),
        vmem((rows, HEAD), F32),
        vmem((HEAD, 2 * rows), F32),
        vmem((HEAD, 2 * rows), BF16),
        vmem((rows, HEAD), BF16),
        vmem((REACH, 2, rows, HEAD), BF16),
        vmem((REACH, 2, rows, HEAD), BF16),
        vmem((2 * HEAD, rows), BF16),
        vmem((n_tp, 2 * HEAD, chunk), BF16),
        vmem((2 * HEAD, rows), BF16),
        vmem((2 * HEAD, rows), BF16),
        vmem((n_tp, 2 * HEAD, chunk), BF16),
        vmem((2 * HEAD, rows), BF16),
        vmem((total, HEAD), F32),
        vmem((half, HEAD), BF16),
        vmem((half, HEAD), BF16),
        vmem((half, HEAD), BF16),
        vmem((pairs, piece, HEAD), BF16),
        vmem((total, HEAD), BF16),
        dma((3, REACH)),
        dma((3, REACH)),
        dma((REACH,)),
        dma((REACH,)),
        dma((6, n_tp)),
        dma((6, n_tp)),
        dma((2,)),
        dma((2,)),
        dma((2, pairs)),
        dma((2, pairs)),
    ]
    whole = pl.BlockSpec(memory_space=pltpu.VMEM)
    flops = 10 * 9 * rows * rows * HEAD
    return pl.pallas_call(
        functools.partial(kernel, n_ctx, n_tp),
        out_shape=[
            jax.ShapeDtypeStruct((rows, HEAD), BF16),
            jax.ShapeDtypeStruct((width, HEAD), F32),
            jax.ShapeDtypeStruct((HEAD, 2 * HEAD), F32),
            jax.ShapeDtypeStruct((width, HEAD), F32),
            jax.ShapeDtypeStruct((HEAD, HEAD), F32),
        ],
        in_specs=[whole] * 12,
        out_specs=[whole] * 5,
        scratch_shapes=scratch,
        compiler_params=pltpu.CompilerParams(
            collective_id=0, has_side_effects=True, vmem_limit_bytes=56 * 1024 * 1024
        ),
        cost_estimate=pl.CostEstimate(
            flops=flops, bytes_accessed=8 * 1024 * 1024, transcendentals=9 * rows * rows
        ),
    )(x, q, k, v, do, o, lse, seg.reshape(1, rows), aq, bq, av, bv)


def solution(mesh):
    placed = (
        P("ctx", "tp"),
        P("ctx", "tp"),
        P("ctx", "tp"),
        P("ctx", "tp"),
        P("ctx", "tp"),
        P("ctx", "tp"),
        P("tp", "ctx"),
        P("ctx"),
        P("tp", None),
        P(None, "tp"),
        P("tp", None),
        P(None, "tp"),
    )
    return jax.shard_map(
        per_device,
        mesh=mesh,
        in_specs=placed,
        out_specs=(P("ctx", "tp"), P("tp", None), P(None, "tp"), P("tp", None), P(None, "tp")),
        check_vma=False,
    )
```

time: 550 us -> 135 us (0.25); the launches traced: 542 us -> 134 us
  waiting for transfers between devices: 280 us -> 0 us
  Pallas kernels: 0 us -> 125 us
  blocking collectives: 86.8 us -> 0 us
  matrix products: 78.5 us -> 0 us
  starting transfers between devices: 60.9 us -> 0 us
  between operations: 15.1 us -> 0.66 us
  other arithmetic: 11 us -> 0 us
    psum x1 -> x0, waiting for transfers between devices: 277 us -> none  [per_device(): lax.psum((grad_a_query, grad_b_query, grad_a_value, grad_b_value), 'ctx')]
    pallas_call x0 -> x1, Pallas kernels: none -> 125 us  [per_device(): pl.pallas_call(functools.partial(kernel, n_ctx, n_tp), out_shape=[jax.Sha...]
    psum x1 -> x0, blocking collectives: 86.8 us -> none  [per_device(): lax.psum((query_adapter_output, value_adapter_output), 'tp')]
    dot_general x33 -> x0, matrix products: 78.5 us -> none  [the longest x5 19.9 us: per_device(): jnp.einsum('ikgd,jkd->kgij', grad_heads, value_heads, preferred_element_t...]
    ppermute x20 -> x0, starting transfers between devices: 60.8 us -> none  [passed_along(): lax.ppermute(value, axis, [(source, source + steps) for source in range(f...]
    and x1 -> x0, other arithmetic: 8.43 us -> none  [per_device(): (distance >= 0) & (distance < WINDOW)]
  transfers between devices with their start and end apart: 21 -> 0, of which waited for: 3 -> 0; matrix products, arithmetic and copies ran while one was open for 17% -> 0% of each run, Pallas kernels for 0% -> 0%
where the time goes in v1:
time: 135 us; the launch traced here: 134 us
  Pallas kernels  125 us (93%)
  local copies, waits for them, and re-layouts  8.74 us (6%)
    pallas_call x1, Pallas kernels, per_device(): pl.pallas_call(functools.partial(kernel, n_ctx, n_tp), out_shape=[jax.Sha...  125 us
    unnamed x10, local copies, waits for them, and re-layouts  8.74 us

profile of v1, /device:TPU:1, one launch (start us, length us, event | category | flops | bytes accessed | tf_op | source)
XLA Modules:
  0.0 134.4 jit_solution(1833432676241233650)
XLA Ops:
  0.6 2.4 %copy.17.x_ref = bf16[1024,576]{1,0:T(8,128)(2,1)} copy(bf16[1024,576]{0,1:T(8,128)(2,1)} %param.12) | data formatting | bytes 2359296 | tf_op args[0]
  3.0 125.0 %shard_map.155 = (bf16[1024,128]{1,0:T(8,128)(2,1)}, f32[576,128]{1,0:T(8,128)}, f32[128,256]{1,0:T(8,128)}, f32[576,128]{1,0:T(8,128)}, f32[128,128]{1,0:T(8,128)}) custom-call(bf16[1024,576]{1,0:T(8,128)(2,1)} %copy.17.x_ref, bf16[1024,256]{1,0:T(8,128)(2,1)} %q_ref.1, bf16[1024,128]{1,0:T(8,128)(2,1)} %k_ref.1, bf16[1024,128]{1,0:T(8,128)(2,1)} %v_ref.1, ...), custom_call_target="tpu_custom_call" | custom-call | flops 12079595520 | bytes 8388608 | tf_op jit(solution)/shard_map/pallas_call | solution.py:445
  128.0 0.0 copy-start
  128.0 0.0 copy-start.1
  128.0 1.7 %copy.23 = bf16[1024,128]{1,0:T(8,128)(2,1)} copy(bf16[1024,128]{1,0:T(8,128)(2,1)} %get-tuple-element.10) | data formatting | bytes 524288
  129.8 1.7 %copy.24 = f32[576,128]{1,0:T(8,128)} copy(f32[576,128]{1,0:T(8,128)} %get-tuple-element.11) | data formatting | bytes 589824
  131.5 1.6 %copy.25 = f32[128,256]{1,0:T(8,128)} copy(f32[128,256]{1,0:T(8,128)} %get-tuple-element.12) | data formatting | bytes 262144
  133.0 0.0 copy-done
  133.0 0.7 copy.26
  133.7 0.0 copy-done.1
  133.7 0.6 copy.27
Async XLA Ops:
  128.0 5.0 %copy-start = (f32[576,128]{1,0:T(8,128)S(1)}, f32[576,128]{1,0:T(8,128)}, u32[]{:S(2)}) copy-start(f32[576,128]{1,0:T(8,128)} %get-tuple-element.13) | copy-start | bytes 884740
  128.0 5.7 %copy-start.1 = (f32[128,128]{1,0:T(8,128)S(1)}, f32[128,128]{1,0:T(8,128)}, u32[]{:S(2)}) copy-start(f32[128,128]{1,0:T(8,128)} %get-tuple-element.14) | copy-start | bytes 196612

commit v2 on v1

--- a/solution.py
+++ b/solution.py
@@ -27,6 +27,20 @@
 def kernel(
     n_ctx,
     n_tp,
+    x_hbm,
+    q_hbm,
+    k_hbm,
+    v_hbm,
+    do_hbm,
+    o_hbm,
+    lse_hbm,
+    seg_hbm,
+    aq_hbm,
+    bq_hbm,
+    av_hbm,
+    bv_hbm,
+    key_grad_ref,
+    sums_ref,
     x_ref,
     q_ref,
     k_ref,
@@ -39,11 +53,7 @@
     bq_ref,
     av_ref,
     bv_ref,
-    key_grad_ref,
-    ga_q_ref,
-    gb_q_ref,
-    ga_v_ref,
-    gb_v_ref,
+    load_sem,
     k_in,
     v_in,
     seg_in,
@@ -52,10 +62,8 @@
     lse_st,
     delta_st,
     thr_st,
-    dk_acc,
-    dv_acc,
-    dk_own,
-    dv_own,
+    acc,
+    own,
     dq_acc,
     dq_low,
     dv_low,
@@ -85,7 +93,7 @@
     piece_recv,
 ):
     rows = k_ref.shape[0]
-    width = x_ref.shape[1]
+    width = x_ref.shape[0]
     chunk = rows // n_tp
     pairs = n_ctx // 2
     total = g_all.shape[0]
@@ -95,6 +103,7 @@
     t = lax.axis_index("tp")
     core = lax.rem(c, 2)
     pair = c // 2
+    side = lax.rem(pair, 2)
 
     def ctx_at(offset):
         return lax.rem(c + (offset + n_ctx), n_ctx)
@@ -113,36 +122,65 @@
         pl.semaphore_signal(
             barrier, inc=1, device_id={"tp": tp_at(offset)}, device_id_type=MESH
         )
+    loads = {}
+    for place, (src, dst) in enumerate(
+        (
+            (k_hbm, k_ref),
+            (v_hbm, v_ref),
+            (seg_hbm, seg_ref),
+            (aq_hbm, aq_ref),
+            (av_hbm, av_ref),
+            (x_hbm, x_ref),
+            (q_hbm, q_ref),
+            (do_hbm, do_ref),
+            (o_hbm, o_ref),
+            (lse_hbm, lse_ref),
+            (bq_hbm, bq_ref),
+            (bv_hbm, bv_ref),
+        )
+    ):
+        loads[place] = pltpu.make_async_copy(src, dst, load_sem.at[place])
+        loads[place].start()
+    for place in range(6):
+        loads[place].wait()
+    low_s[0:HEAD, :] = contract(aq_ref[...], x_ref[...], 0, 0).astype(BF16)
+    low_s[HEAD : 2 * HEAD, :] = contract(av_ref[...], x_ref[...], 0, 0).astype(BF16)
     pl.semaphore_wait(barrier, len(offsets) + n_tp - 1)
 
-    def kv_copies(step):
-        found = []
-        for which, (src, dst) in enumerate(
-            ((k_ref, k_in), (v_ref, v_in), (seg_ref, seg_in))
-        ):
-            found.append(
-                pltpu.make_async_remote_copy(
-                    src_ref=src,
-                    dst_ref=dst.at[step - 1],
-                    send_sem=kv_send.at[which, step - 1],
-                    recv_sem=kv_recv.at[which, step - 1],
-                    device_id={"ctx": ctx_at(step)},
-                    device_id_type=MESH,
-                )
-            )
-        return found
-
-    for step in range(1, REACH + 1):
-        for copy in kv_copies(step):
-            copy.start()
-
-    def part_copy(step):
-        return pltpu.make_async_remote_copy(
-            src_ref=part_out.at[step - 1],
-            dst_ref=part_in.at[step - 1],
-            send_sem=part_send.at[step - 1],
-            recv_sem=part_recv.at[step - 1],
-            device_id={"ctx": ctx_at(-step)},
+    cross_core = c + 1 - 2 * core
+    cross_x = c + 2 - 4 * side
+    sources = (seg_ref, k_ref, v_ref)
+    landed = (seg_in, k_in, v_in)
+
+    def kv_copy(which, slot, target, relay=None):
+        src = sources[which] if relay is None else landed[which].at[relay]
+        return pltpu.make_async_remote_copy(
+            src_ref=src,
+            dst_ref=landed[which].at[slot],
+            send_sem=kv_send.at[which, slot],
+            recv_sem=kv_recv.at[which, slot],
+            device_id={"ctx": target},
+            device_id_type=MESH,
+        )
+
+    for which in range(3):
+        kv_copy(which, 0, ctx_at(REACH)).start()
+
+        @pl.when(core == 0)
+        def _(which=which):
+            kv_copy(which, 1, cross_core).start()
+
+        @pl.when(side == 0)
+        def _(which=which):
+            kv_copy(which, 2, cross_x).start()
+
+    def part_copy(slot, which, target):
+        return pltpu.make_async_remote_copy(
+            src_ref=part_out.at[slot, which],
+            dst_ref=part_in.at[slot, which],
+            send_sem=part_send.at[slot, which],
+            recv_sem=part_recv.at[slot, which],
+            device_id={"ctx": target},
             device_id_type=MESH,
         )
 
@@ -188,9 +226,9 @@
         for offset in range(1, n_tp):
             gather_copy(which + 1, ref, first, high, offset).wait()
 
-    low_s[0:HEAD, :] = contract(aq_ref[...], x_ref[...], 0, 1).astype(BF16)
-    low_s[HEAD : 2 * HEAD, :] = contract(av_ref[...], x_ref[...], 0, 1).astype(BF16)
     scatter_start(0, low_s, low_r, 0, 2 * HEAD)
+    for place in range(6, 12):
+        loads[place].wait()
 
     ones = jnp.ones((8, HEAD), BF16)
     for h in range(HEADS_LOCAL):
@@ -218,7 +256,7 @@
         for h in range(HEADS_LOCAL):
             thr_st[:, h * rows : (h + 1) * rows] = found
 
-    def tile(keys, values, sum_k, sum_v, k0, kt, r0, rt, causal):
+    def tile(keys, values, sums, k0, kt, r0, rt, causal):
         ks, rs = slice(k0, k0 + kt), slice(r0, r0 + rt)
         key, value = keys[ks, :], values[ks, :]
         query, grad = q_st[rs, :], do_st[rs, :]
@@ -231,57 +269,86 @@
         dprob = contract(value, grad, 1, 1)
         prob = jnp.where(mask, jnp.exp2(score * (SCORE_SCALE * LOG2E) - lse_st[:, rs]), 0.0)
         dscore = (prob * (dprob - delta_st[:, rs])).astype(BF16)
-        sum_v[ks, :] += contract(prob.astype(BF16), grad, 1, 0)
-        sum_k[ks, :] += contract(dscore, query, 1, 0)
+        sums[0, ks, :] += contract(prob.astype(BF16), grad, 1, 0)
+        sums[1, ks, :] += contract(dscore, query, 1, 0)
         dq_acc[:, rs] += contract(key, dscore, 0, 0)
 
     edge = min(256, rows)
     wide = min(512, rows)
 
     dq_acc[...] = jnp.zeros_like(dq_acc)
-    dk_own[...] = jnp.zeros_like(dk_own)
-    dv_own[...] = jnp.zeros_like(dv_own)
+    own[...] = jnp.zeros_like(own)
+    acc[0] = jnp.zeros_like(own)
     set_thr(first_allowed(seg_ref[...], True))
     for h in range(HEADS_LOCAL):
         for r in range(0, rows, edge):
             if r:
-                tile(k_ref, v_ref, dk_own, dv_own, 0, r, h * rows + r, edge, False)
-            tile(k_ref, v_ref, dk_own, dv_own, r, edge, h * rows + r, edge, True)
+                tile(k_ref, v_ref, own, 0, r, h * rows + r, edge, False)
+            tile(k_ref, v_ref, own, r, edge, h * rows + r, edge, True)
 
     scatter_finish(0, low_s, low_r, low_g, 0, 2 * HEAD)
 
-    def open_step(step):
-        for copy in kv_copies(step):
-            copy.wait()
-        dk_acc[...] = jnp.zeros_like(dk_acc)
-        dv_acc[...] = jnp.zeros_like(dv_acc)
-        return first_allowed(seg_in[step - 1], c >= step)
-
-    def close_step(step):
-        part_out[step - 1, 0] = (SCORE_SCALE * dk_acc[...]).astype(BF16)
-        part_out[step - 1, 1] = dv_acc[...].astype(BF16)
-        part_copy(step).start()
-
-    def full_step(step, carry):
-        set_thr(open_step(step))
-        keys, values = k_in.at[step - 1], v_in.at[step - 1]
-        for r in range(0, HEADS_LOCAL * rows, wide):
-            for k0 in range(0, rows, wide):
-                tile(keys, values, dk_acc, dv_acc, k0, wide, r, wide, False)
-        close_step(step)
-        return carry
-
-    lax.fori_loop(1, REACH, full_step, 0)
+    for which in range(3):
+        kv_copy(which, 0, cross_core).wait_recv()
+
+        @pl.when(core == 1)
+        def _(which=which):
+            kv_copy(which, 1, cross_core, 0).start()
+
+        @pl.when(side == 1)
+        def _(which=which):
+            kv_copy(which, 2, cross_x, 0).start()
 
     i = lax.broadcasted_iota(jnp.int32, (1, rows), 1)
-    set_thr(jnp.maximum(open_step(REACH), i + 1))
+    set_thr(jnp.maximum(first_allowed(seg_in[0], c >= REACH), i + 1))
     for h in range(HEADS_LOCAL):
         for r in range(0, rows, edge):
             tile(
-                k_in.at[REACH - 1], v_in.at[REACH - 1], dk_acc, dv_acc,
-                r, rows - r, h * rows + r, edge, False,
+                k_in.at[0], v_in.at[0], acc.at[0], r, rows - r, h * rows + r, edge, False
             )
-    close_step(REACH)
+
+    def full_step(slot, carry):
+        for which in range(3):
+            kv_copy(which, slot, cross_core).wait_recv()
+
+        @pl.when(slot == 2)
+        def _():
+            for which in range(3):
+                kv_copy(which, 3, cross_core, 2).start()
+
+        back = jnp.where(slot == 2, 2, jnp.where((slot == 1) == (core == 1), 1, 3))
+        set_thr(first_allowed(seg_in[slot], c >= back))
+        sums = acc.at[2 - lax.rem(slot, 2)]
+        sums[...] = jnp.zeros_like(own)
+        keys, values = k_in.at[slot], v_in.at[slot]
+        for r in range(0, HEADS_LOCAL * rows, wide):
+            for k0 in range(0, rows, wide):
+                tile(keys, values, sums, k0, wide, r, wide, False)
+
+        @pl.when(slot != 2)
+        def _():
+            part_out[slot, 0] = acc[1, 0].astype(BF16)
+            part_copy(slot, 0, cross_core).start()
+            part_out[slot, 1] = (SCORE_SCALE * acc[1, 1]).astype(BF16)
+            part_copy(slot, 1, cross_core).start()
+
+        @pl.when(slot == 2)
+        def _():
+            for which in range(2):
+                part_copy(1, which, cross_core).wait()
+            second = core == 1
+            acc[0, 0] = acc[0, 0] + jnp.where(second, part_in[1, 0].astype(F32), 0.0)
+            acc[0, 1] = SCORE_SCALE * acc[0, 1] + jnp.where(
+                second, part_in[1, 1].astype(F32), 0.0
+            )
+
+            for which in range(2):
+                part_out[0, which] = acc[0, which].astype(BF16)
+                part_copy(0, which, ctx_at(-REACH)).start()
+
+        return carry
+
+    lax.fori_loop(1, REACH, full_step, 0)
 
     token_scale = 1.0 / math.sqrt(rows * n_ctx)
 
@@ -291,6 +358,10 @@
         + contract(bq_ref[:, HEAD : 2 * HEAD], dq_low[:, rows : 2 * rows], 1, 0)
     ).astype(BF16)
     scatter_start(2, back_s, back_r, 0, HEAD)
+    part_copy(3, 0, cross_core).wait()
+    part_out[2, 0] = (acc[2, 0] + part_in[3, 0].astype(F32)).astype(BF16)
+    part_copy(2, 0, ctx_at(-2)).start()
+
     gather_finish(0, low_g, 0, 2 * HEAD)
     base = 2 * width
     for h in range(HEADS_LOCAL):
@@ -299,26 +370,28 @@
         )
     scatter_finish(2, back_s, back_r, back_g, 0, HEAD)
 
-    dk_sum = SCORE_SCALE * dk_own[...]
-    dv_sum = dv_own[...]
-    for step in range(1, REACH + 1):
-        part_copy(step).wait()
-        dv_sum = dv_sum + part_in[step - 1, 1].astype(F32)
-    dv_low[...] = dv_sum.astype(BF16)
+    def gathered(which):
+        near = jnp.where(core == 0, part_in[1, which].astype(F32), 0.0)
+        part_copy(0, which, ctx_at(-REACH)).wait()
+        part_copy(2, which, ctx_at(-2)).wait()
+        return near + part_in[0, which].astype(F32) + part_in[2, which].astype(F32)
+
+    dv_low[...] = (own[0] + gathered(0)).astype(BF16)
     back_s[HEAD : 2 * HEAD, :] = contract(bv_ref[...], dv_low[...], 1, 1).astype(BF16)
     scatter_start(4, back_s, back_r, HEAD, HEAD)
-    for step in range(1, REACH + 1):
-        dk_sum = dk_sum + part_in[step - 1, 0].astype(F32)
-    key_grad_ref[...] = dk_sum.astype(BF16)
+    part_copy(3, 1, cross_core).wait()
+    part_out[2, 1] = (SCORE_SCALE * acc[2, 1] + part_in[3, 1].astype(F32)).astype(BF16)
+    part_copy(2, 1, ctx_at(-2)).start()
     g_all[total - HEAD : total, :] = token_scale * contract(
         low_g[HEAD : 2 * HEAD, :], dv_low[...], 1, 0
     )
     gather_finish(2, back_g, 0, HEAD)
-    g_all[0:width, :] = token_scale * contract(back_g[0:HEAD, :], x_ref[...], 1, 0).T
+    g_all[0:width, :] = token_scale * contract(x_ref[...], back_g[0:HEAD, :], 1, 1)
+
     scatter_finish(4, back_s, back_r, back_g, HEAD, HEAD)
     gather_finish(4, back_g, HEAD, HEAD)
-    g_all[width : 2 * width, :] = (
-        token_scale * contract(back_g[HEAD : 2 * HEAD, :], x_ref[...], 1, 0).T
+    g_all[width : 2 * width, :] = token_scale * contract(
+        x_ref[...], back_g[HEAD : 2 * HEAD, :], 1, 1
     )
 
     other = 1 - core
@@ -380,13 +453,24 @@
     swap.start()
     swap.wait()
 
-    ga_q_ref[...] = g_out[0:width, :].astype(F32)
-    ga_v_ref[...] = g_out[width : 2 * width, :].astype(F32)
+    sums_ref[...] = g_out[...]
+    key_grad_ref[...] = (SCORE_SCALE * own[1] + gathered(1)).astype(BF16)
+    for which in range(3):
+        for slot in range(REACH):
+            kv_copy(which, slot, cross_core).wait_send()
+
+
+def finish(key_ref, sums_ref, key_grad_ref, ga_q_ref, gb_q_ref, ga_v_ref, gb_v_ref):
+    key_grad_ref[...] = key_ref[...]
+    width = ga_q_ref.shape[0]
+    base = 2 * width
+    ga_q_ref[...] = sums_ref[0:width, :].astype(F32)
+    ga_v_ref[...] = sums_ref[width : 2 * width, :].astype(F32)
     for h in range(HEADS_LOCAL):
         gb_q_ref[:, h * HEAD : (h + 1) * HEAD] = (
-            g_out[base + h * HEAD : base + (h + 1) * HEAD, :].astype(F32).T
-        )
-    gb_v_ref[...] = g_out[total - HEAD : total, :].astype(F32)
+            sums_ref[base + h * HEAD : base + (h + 1) * HEAD, :].astype(F32).T
+        )
+    gb_v_ref[...] = sums_ref[base + HEADS_LOCAL * HEAD :, :].astype(F32)
 
 
 def per_device(x, q, k, v, do, o, lse, seg, aq, bq, av, bv):
@@ -400,6 +484,19 @@
     dma = pltpu.SemaphoreType.DMA
     vmem = pltpu.VMEM
     scratch = [
+        vmem((width, rows), BF16),
+        vmem((rows, 2 * HEAD), BF16),
+        vmem((rows, HEAD), BF16),
+        vmem((rows, HEAD), BF16),
+        vmem((rows, 2 * HEAD), BF16),
+        vmem((rows, 2 * HEAD), BF16),
+        vmem((2, rows), F32),
+        vmem((1, rows), jnp.int32),
+        vmem((width, HEAD), BF16),
+        vmem((HEAD, 2 * HEAD), BF16),
+        vmem((width, HEAD), BF16),
+        vmem((HEAD, HEAD), BF16),
+        dma((12,)),
         vmem((REACH, rows, HEAD), BF16),
         vmem((REACH, rows, HEAD), BF16),
         vmem((REACH, 1, rows), jnp.int32),
@@ -408,10 +505,8 @@
         vmem((1, 2 * rows), F32),
         vmem((1, 2 * rows), F32),
         vmem((1, 2 * rows), jnp.int32),
-        vmem((rows, HEAD), F32),
-        vmem((rows, HEAD), F32),
-        vmem((rows, HEAD), F32),
-        vmem((rows, HEAD), F32),
+        vmem((3, 2, rows, HEAD), F32),
+        vmem((2, rows, HEAD), F32),
         vmem((HEAD, 2 * rows), F32),
         vmem((HEAD, 2 * rows), BF16),
         vmem((rows, HEAD), BF16),
@@ -431,8 +526,8 @@
         vmem((total, HEAD), BF16),
         dma((3, REACH)),
         dma((3, REACH)),
-        dma((REACH,)),
-        dma((REACH,)),
+        dma((REACH, 2)),
+        dma((REACH, 2)),
         dma((6, n_tp)),
         dma((6, n_tp)),
         dma((2,)),
@@ -442,8 +537,24 @@
     ]
     whole = pl.BlockSpec(memory_space=pltpu.VMEM)
     flops = 10 * 9 * rows * rows * HEAD
+    key_grad, sums = pl.pallas_call(
+        functools.partial(kernel, n_ctx, n_tp),
+        out_shape=[
+            jax.ShapeDtypeStruct((rows, HEAD), BF16),
+            jax.ShapeDtypeStruct((total, HEAD), BF16),
+        ],
+        in_specs=[pl.BlockSpec(memory_space=pl.ANY)] * 12,
+        out_specs=[whole] * 2,
+        scratch_shapes=scratch,
+        compiler_params=pltpu.CompilerParams(
+            collective_id=0, has_side_effects=True, vmem_limit_bytes=56 * 1024 * 1024
+        ),
+        cost_estimate=pl.CostEstimate(
+            flops=flops, bytes_accessed=8 * 1024 * 1024, transcendentals=9 * rows * rows
+        ),
+    )(x.T, q, k, v, do, o, lse, seg.reshape(1, rows), aq, bq, av, bv)
     return pl.pallas_call(
-        functools.partial(kernel, n_ctx, n_tp),
+        finish,
         out_shape=[
             jax.ShapeDtypeStruct((rows, HEAD), BF16),
             jax.ShapeDtypeStruct((width, HEAD), F32),
@@ -451,16 +562,9 @@
             jax.ShapeDtypeStruct((width, HEAD), F32),
             jax.ShapeDtypeStruct((HEAD, HEAD), F32),
         ],
-        in_specs=[whole] * 12,
+        in_specs=[whole] * 2,
         out_specs=[whole] * 5,
-        scratch_shapes=scratch,
-        compiler_params=pltpu.CompilerParams(
-            collective_id=0, has_side_effects=True, vmem_limit_bytes=56 * 1024 * 1024
-        ),
-        cost_estimate=pl.CostEstimate(
-            flops=flops, bytes_accessed=8 * 1024 * 1024, transcendentals=9 * rows * rows
-        ),
-    )(x, q, k, v, do, o, lse, seg.reshape(1, rows), aq, bq, av, bv)
+    )(key_grad, sums)
 
 
 def solution(mesh):

time: 135 us -> 107 us (0.79)
  Pallas kernels: 125 us -> 106 us
  local copies, waits for them, and re-layouts: 8.74 us -> 0 us
    pallas_call x1, Pallas kernels: 125 us -> 104 us  [per_device(): pl.pallas_call(functools.partial(kernel, n_ctx, n_tp), out_shape=[jax.Sha...]
    unnamed x10 -> x0, local copies, waits for them, and re-layouts: 8.74 us -> none
    pallas_call x0 -> x1, Pallas kernels: none -> 2.07 us  [per_device(): pl.pallas_call(finish, out_shape=[jax.ShapeDtypeStruct((rows, HEAD), BF16...]
where the time goes in v2:
time: 107 us
  Pallas kernels  106 us (99%)
    pallas_call x1, Pallas kernels, per_device(): pl.pallas_call(functools.partial(kernel, n_ctx, n_tp), out_shape=[jax.Sha...  104 us

profile of v2, /device:TPU:1, one launch (start us, length us, event | category | flops | bytes accessed | tf_op | source)
XLA Modules:
  0.0 107.0 jit_solution(15029775370883482817)
XLA Ops:
  0.6 104.3 %shard_map.155 = (bf16[1024,128]{1,0:T(8,128)(2,1)}, bf16[1536,128]{1,0:T(8,128)(2,1)}) custom-call(bf16[576,1024]{1,0:T(8,128)(2,1)} %bitcast.2, bf16[1024,256]{1,0:T(8,128)(2,1)} %q_hbm.1, bf16[1024,128]{1,0:T(8,128)(2,1)} %k_hbm.1, bf16[1024,128]{1,0:T(8,128)(2,1)} %v_hbm.1, bf16[1024,256]{1,0:T(8,128)(2,1)} %do_hbm.1, bf16[1024,256]{1,0:T(8,128)(2,1)} %o_hbm.1, ...), custom_call_target="tpu_custom_call" | custom-call | flops 12079595520 | bytes 8388608 | tf_op jit(solution)/shard_map/pallas_call | solution.py:540
  104.9 2.1 %shard_map.156 = (bf16[1024,128]{1,0:T(8,128)(2,1)}, f32[576,128]{1,0:T(8,128)}, f32[128,256]{1,0:T(8,128)}, f32[576,128]{1,0:T(8,128)}, f32[128,128]{1,0:T(8,128)}) custom-call(bf16[1024,128]{1,0:T(8,128)(2,1)} %get-tuple-element.7.key_ref, bf16[1536,128]{1,0:T(8,128)(2,1)} %get-tuple-element.8.sums_ref), custom_call_target="tpu_custom_call" | custom-call | tf_op jit(solution)/shard_map/pallas_call | solution.py:556

commit v3 on v2

--- a/solution.py
+++ b/solution.py
@@ -149,21 +149,30 @@
 
     cross_core = c + 1 - 2 * core
     cross_x = c + 2 - 4 * side
-    sources = (seg_ref, k_ref, v_ref)
-    landed = (seg_in, k_in, v_in)
+    mid = rows // 2
+    pieces = ((seg_ref, seg_in, None), (k_ref, k_in, 0), (v_ref, v_in, 0), (k_ref, k_in, 1), (v_ref, v_in, 1))
+    groups = ((0, 1, 2), (3, 4))
 
     def kv_copy(which, slot, target, relay=None):
-        src = sources[which] if relay is None else landed[which].at[relay]
+        src, dst, part = pieces[which]
+        src = src if relay is None else dst.at[relay]
+        dst = dst.at[slot]
+        if part is not None:
+            src, dst = src.at[pl.ds(part * mid, mid)], dst.at[pl.ds(part * mid, mid)]
         return pltpu.make_async_remote_copy(
             src_ref=src,
-            dst_ref=landed[which].at[slot],
+            dst_ref=dst,
             send_sem=kv_send.at[which, slot],
             recv_sem=kv_recv.at[which, slot],
             device_id={"ctx": target},
             device_id_type=MESH,
         )
 
-    for which in range(3):
+    def arrived(slot, part):
+        for which in groups[part]:
+            kv_copy(which, slot, cross_core).wait_recv()
+
+    for which in range(5):
         kv_copy(which, 0, ctx_at(REACH)).start()
 
         @pl.when(core == 0)
@@ -174,12 +183,29 @@
         def _(which=which):
             kv_copy(which, 2, cross_x).start()
 
-    def part_copy(slot, which, target):
+    def hand_on(part):
+        for which in groups[part]:
+            kv_copy(which, 0, cross_core).wait_recv()
+
+            @pl.when(core == 1)
+            def _(which=which):
+                kv_copy(which, 1, cross_core, 0).start()
+
+            @pl.when(side == 1)
+            def _(which=which):
+                kv_copy(which, 2, cross_x, 0).start()
+
+    def part_copy(slot, which, target, part=None):
+        src, dst = part_out.at[slot, which], part_in.at[slot, which]
+        place = 2 * which
+        if part is not None:
+            src, dst = src.at[pl.ds(part * mid, mid)], dst.at[pl.ds(part * mid, mid)]
+            place = place + part
         return pltpu.make_async_remote_copy(
-            src_ref=part_out.at[slot, which],
-            dst_ref=part_in.at[slot, which],
-            send_sem=part_send.at[slot, which],
-            recv_sem=part_recv.at[slot, which],
+            src_ref=src,
+            dst_ref=dst,
+            send_sem=part_send.at[slot, place],
+            recv_sem=part_recv.at[slot, place],
             device_id={"ctx": target},
             device_id_type=MESH,
         )
@@ -226,7 +252,6 @@
         for offset in range(1, n_tp):
             gather_copy(which + 1, ref, first, high, offset).wait()
 
-    scatter_start(0, low_s, low_r, 0, 2 * HEAD)
     for place in range(6, 12):
         loads[place].wait()
 
@@ -257,7 +282,7 @@
             thr_st[:, h * rows : (h + 1) * rows] = found
 
     def tile(keys, values, sums, k0, kt, r0, rt, causal):
-        ks, rs = slice(k0, k0 + kt), slice(r0, r0 + rt)
+        ks, rs = pl.ds(k0, kt), pl.ds(r0, rt)
         key, value = keys[ks, :], values[ks, :]
         query, grad = q_st[rs, :], do_st[rs, :]
         j = lax.broadcasted_iota(jnp.int32, (kt, rt), 0) + k0
@@ -286,18 +311,21 @@
                 tile(k_ref, v_ref, own, 0, r, h * rows + r, edge, False)
             tile(k_ref, v_ref, own, r, edge, h * rows + r, edge, True)
 
-    scatter_finish(0, low_s, low_r, low_g, 0, 2 * HEAD)
-
-    for which in range(3):
-        kv_copy(which, 0, cross_core).wait_recv()
-
-        @pl.when(core == 1)
-        def _(which=which):
-            kv_copy(which, 1, cross_core, 0).start()
-
-        @pl.when(side == 1)
-        def _(which=which):
-            kv_copy(which, 2, cross_x, 0).start()
+    def half_block(slot, part):
+        back = jnp.where(slot == 2, 2, jnp.where((slot == 1) == (core == 1), 1, 3))
+        set_thr(first_allowed(seg_in[slot], c >= back))
+        k0 = pl.multiple_of(part * mid, mid)
+        sums = acc.at[2 - slot % 2]
+        for which in range(2):
+            sums[which, pl.ds(k0, mid), :] = jnp.zeros((mid, HEAD), F32)
+        for r in range(0, HEADS_LOCAL * rows, wide):
+            tile(k_in.at[slot], v_in.at[slot], sums, k0, mid, r, wide, False)
+
+    hand_on(0)
+    arrived(1, 0)
+    half_block(1, 0)
+    hand_on(1)
+    scatter_start(0, low_s, low_r, 0, 2 * HEAD)
 
     i = lax.broadcasted_iota(jnp.int32, (1, rows), 1)
     set_thr(jnp.maximum(first_allowed(seg_in[0], c >= REACH), i + 1))
@@ -307,48 +335,92 @@
                 k_in.at[0], v_in.at[0], acc.at[0], r, rows - r, h * rows + r, edge, False
             )
 
-    def full_step(slot, carry):
-        for which in range(3):
-            kv_copy(which, slot, cross_core).wait_recv()
-
-        @pl.when(slot == 2)
-        def _():
-            for which in range(3):
+    scales = (1.0, SCORE_SCALE)
+
+    def send_last(part):
+        span = slice(part * mid, (part + 1) * mid)
+        for which in range(2):
+            part_out[3, which, span] = (scales[which] * acc[1, which, span]).astype(BF16)
+            part_copy(3, which, cross_core, part).start()
+
+    def send_across(part, which):
+        span = slice(part * mid, (part + 1) * mid)
+        part_copy(3, which, cross_core, part).wait()
+        part_out[2, which, span] = (
+            scales[which] * acc[2, which, span] + part_in[3, which, span].astype(F32)
+        ).astype(BF16)
+        part_copy(2, which, ctx_at(-2), part).start()
+
+    def half_step(step, carry):
+        @pl.when(step == 0)
+        def _():
+            arrived(1, 1)
+
+        @pl.when(step == 1)
+        def _():
+            arrived(2, 0)
+            for which in groups[0]:
                 kv_copy(which, 3, cross_core, 2).start()
 
-        back = jnp.where(slot == 2, 2, jnp.where((slot == 1) == (core == 1), 1, 3))
-        set_thr(first_allowed(seg_in[slot], c >= back))
-        sums = acc.at[2 - lax.rem(slot, 2)]
-        sums[...] = jnp.zeros_like(own)
-        keys, values = k_in.at[slot], v_in.at[slot]
-        for r in range(0, HEADS_LOCAL * rows, wide):
-            for k0 in range(0, rows, wide):
-                tile(keys, values, sums, k0, wide, r, wide, False)
-
-        @pl.when(slot != 2)
-        def _():
-            part_out[slot, 0] = acc[1, 0].astype(BF16)
-            part_copy(slot, 0, cross_core).start()
-            part_out[slot, 1] = (SCORE_SCALE * acc[1, 1]).astype(BF16)
-            part_copy(slot, 1, cross_core).start()
-
-        @pl.when(slot == 2)
-        def _():
-            for which in range(2):
-                part_copy(1, which, cross_core).wait()
-            second = core == 1
-            acc[0, 0] = acc[0, 0] + jnp.where(second, part_in[1, 0].astype(F32), 0.0)
-            acc[0, 1] = SCORE_SCALE * acc[0, 1] + jnp.where(
-                second, part_in[1, 1].astype(F32), 0.0
-            )
-
-            for which in range(2):
-                part_out[0, which] = acc[0, which].astype(BF16)
-                part_copy(0, which, ctx_at(-REACH)).start()
+        @pl.when(step == 2)
+        def _():
+            arrived(2, 1)
+            for which in groups[1]:
+                kv_copy(which, 3, cross_core, 2).start()
+            arrived(3, 0)
+
+        @pl.when(step == 4)
+        def _():
+            arrived(3, 1)
+
+        slot = jnp.where(step == 0, 1, 2 + (step + 1) % 2)
+        part = jnp.where(step == 0, 1, (step - 1) // 2)
+        half_block(slot, part)
+
+        @pl.when(step == 0)
+        def _():
+            part_out[1, 0] = acc[1, 0].astype(BF16)
+            part_copy(1, 0, cross_core).start()
+            part_out[1, 1] = (SCORE_SCALE * acc[1, 1]).astype(BF16)
+            part_copy(1, 1, cross_core).start()
+
+            @pl.when(core == 0)
+            def _():
+                part_out[0, 0] = acc[0, 0].astype(BF16)
+                part_copy(0, 0, ctx_at(-REACH)).start()
+                part_out[0, 1] = (SCORE_SCALE * acc[0, 1]).astype(BF16)
+                part_copy(0, 1, ctx_at(-REACH)).start()
+
+        @pl.when(step == 1)
+        def _():
+            part_copy(1, 0, cross_core).wait()
+            part_copy(1, 1, cross_core).wait()
+
+            @pl.when(core == 1)
+            def _():
+                part_out[0, 0] = (acc[0, 0] + part_in[1, 0].astype(F32)).astype(BF16)
+                part_copy(0, 0, ctx_at(-REACH)).start()
+                part_out[0, 1] = (
+                    SCORE_SCALE * acc[0, 1] + part_in[1, 1].astype(F32)
+                ).astype(BF16)
+                part_copy(0, 1, ctx_at(-REACH)).start()
+
+        @pl.when(step == 2)
+        def _():
+            send_last(0)
+
+        @pl.when(step == 3)
+        def _():
+            send_across(0, 0)
+            scatter_finish(0, low_s, low_r, low_g, 0, 2 * HEAD)
+
+        @pl.when(step == 4)
+        def _():
+            send_last(1)
 
         return carry
 
-    lax.fori_loop(1, REACH, full_step, 0)
+    lax.fori_loop(0, 5, half_step, 0)
 
     token_scale = 1.0 / math.sqrt(rows * n_ctx)
 
@@ -358,9 +430,7 @@
         + contract(bq_ref[:, HEAD : 2 * HEAD], dq_low[:, rows : 2 * rows], 1, 0)
     ).astype(BF16)
     scatter_start(2, back_s, back_r, 0, HEAD)
-    part_copy(3, 0, cross_core).wait()
-    part_out[2, 0] = (acc[2, 0] + part_in[3, 0].astype(F32)).astype(BF16)
-    part_copy(2, 0, ctx_at(-2)).start()
+    send_across(1, 0)
 
     gather_finish(0, low_g, 0, 2 * HEAD)
     base = 2 * width
@@ -373,15 +443,15 @@
     def gathered(which):
         near = jnp.where(core == 0, part_in[1, which].astype(F32), 0.0)
         part_copy(0, which, ctx_at(-REACH)).wait()
-        part_copy(2, which, ctx_at(-2)).wait()
+        part_copy(2, which, ctx_at(-2), 0).wait()
+        part_copy(2, which, ctx_at(-2), 1).wait()
         return near + part_in[0, which].astype(F32) + part_in[2, which].astype(F32)
 
     dv_low[...] = (own[0] + gathered(0)).astype(BF16)
     back_s[HEAD : 2 * HEAD, :] = contract(bv_ref[...], dv_low[...], 1, 1).astype(BF16)
     scatter_start(4, back_s, back_r, HEAD, HEAD)
-    part_copy(3, 1, cross_core).wait()
-    part_out[2, 1] = (SCORE_SCALE * acc[2, 1] + part_in[3, 1].astype(F32)).astype(BF16)
-    part_copy(2, 1, ctx_at(-2)).start()
+    send_across(0, 1)
+    send_across(1, 1)
     g_all[total - HEAD : total, :] = token_scale * contract(
         low_g[HEAD : 2 * HEAD, :], dv_low[...], 1, 0
     )
@@ -455,7 +525,7 @@
 
     sums_ref[...] = g_out[...]
     key_grad_ref[...] = (SCORE_SCALE * own[1] + gathered(1)).astype(BF16)
-    for which in range(3):
+    for which in range(5):
         for slot in range(REACH):
             kv_copy(which, slot, cross_core).wait_send()
 
@@ -524,10 +594,10 @@
         vmem((half, HEAD), BF16),
         vmem((pairs, piece, HEAD), BF16),
         vmem((total, HEAD), BF16),
-        dma((3, REACH)),
-        dma((3, REACH)),
-        dma((REACH, 2)),
-        dma((REACH, 2)),
+        dma((5, REACH)),
+        dma((5, REACH)),
+        dma((REACH, 4)),
+        dma((REACH, 4)),
         dma((6, n_tp)),
         dma((6, n_tp)),
         dma((2,)),

time: 107 us -> 101 us (0.944)
  Pallas kernels: 106 us -> 100 us
    pallas_call x1, Pallas kernels: 104 us -> 98 us  [per_device(): pl.pallas_call(functools.partial(kernel, n_ctx, n_tp), out_shape=[jax.Sha...]
where the time goes in v3:
time: 101 us
  Pallas kernels  100 us (99%)
    pallas_call x1, Pallas kernels, per_device(): pl.pallas_call(functools.partial(kernel, n_ctx, n_tp), out_shape=[jax.Sha...  98 us
    pallas_call x1, Pallas kernels, per_device(): pl.pallas_call(finish, out_shape=[jax.ShapeDtypeStruct((rows, HEAD), BF16...  2.07 us

profile of v3, /device:TPU:1, one launch (start us, length us, event | category | flops | bytes accessed | tf_op | source)
XLA Modules:
  0.0 100.7 jit_solution(7157268743251653737)
XLA Ops:
  0.6 98.0 %shard_map.155 = (bf16[1024,128]{1,0:T(8,128)(2,1)}, bf16[1536,128]{1,0:T(8,128)(2,1)}) custom-call(bf16[576,1024]{1,0:T(8,128)(2,1)} %bitcast.2, bf16[1024,256]{1,0:T(8,128)(2,1)} %q_hbm.1, bf16[1024,128]{1,0:T(8,128)(2,1)} %k_hbm.1, bf16[1024,128]{1,0:T(8,128)(2,1)} %v_hbm.1, bf16[1024,256]{1,0:T(8,128)(2,1)} %do_hbm.1, bf16[1024,256]{1,0:T(8,128)(2,1)} %o_hbm.1, ...), custom_call_target="tpu_custom_call" | custom-call | flops 12079595520 | bytes 8388608 | tf_op jit(solution)/shard_map/pallas_call | solution.py:610
  98.6 2.1 %shard_map.156 = (bf16[1024,128]{1,0:T(8,128)(2,1)}, f32[576,128]{1,0:T(8,128)}, f32[128,256]{1,0:T(8,128)}, f32[576,128]{1,0:T(8,128)}, f32[128,128]{1,0:T(8,128)}) custom-call(bf16[1024,128]{1,0:T(8,128)(2,1)} %get-tuple-element.7.key_ref, bf16[1536,128]{1,0:T(8,128)(2,1)} %get-tuple-element.8.sums_ref), custom_call_target="tpu_custom_call" | custom-call | tf_op jit(solution)/shard_map/pallas_call | solution.py:626

commit v4 on v3

--- a/solution.py
+++ b/solution.py
@@ -495,7 +495,8 @@
             device_id_type=MESH,
         )
 
-    for offset in range(1, pairs):
+    far_first = sorted(range(1, pairs), key=lambda offset: abs(2 * offset - pairs))
+    for offset in far_first:
         piece_copy(offset).start()
     summed = g_all[pl.ds(pl.multiple_of(pair * piece, 16), piece), :]
     for offset in range(1, pairs):
@@ -515,7 +516,7 @@
             device_id_type=MESH,
         )
 
-    for offset in range(1, pairs):
+    for offset in far_first:
         spread_copy(offset).start()
     for offset in range(1, pairs):
         spread_copy(offset).wait()

time: 101 us -> 99.8 us (0.988)
  no operation moved by 1% of the time
where the time goes in v4:
time: 99.8 us; the launch traced here: 99.7 us
  Pallas kernels  99.1 us (99%)
    pallas_call x1, Pallas kernels, per_device(): pl.pallas_call(functools.partial(kernel, n_ctx, n_tp), out_shape=[jax.Sha...  97 us
    pallas_call x1, Pallas kernels, per_device(): pl.pallas_call(finish, out_shape=[jax.ShapeDtypeStruct((rows, HEAD), BF16...  2.07 us

profile of v4, /device:TPU:1, one launch (start us, length us, event | category | flops | bytes accessed | tf_op | source)
XLA Modules:
  0.0 99.7 jit_solution(16438788474205099639)
XLA Ops:
  0.6 97.0 %shard_map.155 = (bf16[1024,128]{1,0:T(8,128)(2,1)}, bf16[1536,128]{1,0:T(8,128)(2,1)}) custom-call(bf16[576,1024]{1,0:T(8,128)(2,1)} %bitcast.2, bf16[1024,256]{1,0:T(8,128)(2,1)} %q_hbm.1, bf16[1024,128]{1,0:T(8,128)(2,1)} %k_hbm.1, bf16[1024,128]{1,0:T(8,128)(2,1)} %v_hbm.1, bf16[1024,256]{1,0:T(8,128)(2,1)} %do_hbm.1, bf16[1024,256]{1,0:T(8,128)(2,1)} %o_hbm.1, ...), custom_call_target="tpu_custom_call" | custom-call | flops 12079595520 | bytes 8388608 | tf_op jit(solution)/shard_map/pallas_call | solution.py:611
  97.6 2.1 %shard_map.156 = (bf16[1024,128]{1,0:T(8,128)(2,1)}, f32[576,128]{1,0:T(8,128)}, f32[128,256]{1,0:T(8,128)}, f32[576,128]{1,0:T(8,128)}, f32[128,128]{1,0:T(8,128)}) custom-call(bf16[1024,128]{1,0:T(8,128)(2,1)} %get-tuple-element.7.key_ref, bf16[1536,128]{1,0:T(8,128)(2,1)} %get-tuple-element.8.sums_ref), custom_call_target="tpu_custom_call" | custom-call | tf_op jit(solution)/shard_map/pallas_call | solution.py:627
